TPU v7x, 512 devices: a whole 4x8x8 slice. The times are simulated.
512 devices in a mesh: kx: 8 (over z), ky: 8 (over y_hi, core), kz: 8 (over y_lo, x).
Axes of the slice: x: 4, y: 8 (y_hi: 4, y_lo: 2; y = y_hi * 2 + y_lo), z: 8, core: 2. Of those that a mesh axis runs over, the one named last changes fastest.
Arguments:
- target: bfloat16 [8, 8, 8, 8, 4096], P('kx', 'ky', 'kz'), may hold values from -6 to 6
- target_energy: bfloat16 [8, 8, 8, 8], P('kx', 'ky', 'kz'), may hold values from -1 to 1
- waves: bfloat16 [8, 8, 8, 128, 4096], P('kx', 'ky', 'kz'), may hold values from -6 to 6
- band_energy: float32 [8, 8, 8, 128], P('kx', 'ky', 'kz'), may hold values from -3 to 3
- occupation: int32 [8, 8, 8, 128], P('kx', 'ky', 'kz'), may hold values 0 or 1
- gmap: int32 [3, 4096], replicated, may hold values from 0 to 4095, each once within a row
- pole_vectors: bfloat16 [8, 8, 8, 256, 4096], P('kx', 'ky', 'kz'), may hold values from -0.09375 to 0.09375
- pole_freq: bfloat16 [8, 8, 8, 256], P('kx', 'ky', 'kz'), may hold values from 0.5 to 3
- pole_weight: bfloat16 [8, 8, 8, 256], P('kx', 'ky', 'kz'), may hold values from 0.19921875 to 2
Outputs:
- sigma: float32 [8, 8, 8, 8, 256], P('kx', 'ky', 'kz')
Inputs may be any that keep to these rules, and one draw needn't show every extreme that they name: Each row of gmap is a permutation of 0 to 4095.
All inputs are finite; a program needn't handle non-finite values. No bound on the sum of `occupation` on one device may be relied on, other than what follows from the above.
Results may differ from a plain program's by a relative error of at most 0.00057.
Values may be sent and summed in bfloat16 or wider, within the bound.
A program may use at most 64 MiB of HBM per device.

v0:
```python
import jax
import jax.numpy as jnp
from jax import lax
from jax.sharding import PartitionSpec as P

QSTEPS = ((1, 0, 0), (1, 1, 0), (1, 1, 1))


def as_sent(shard):
    return jax.tree.map(lambda a: a.astype(jnp.bfloat16) if a.dtype == jnp.float32 else a, shard)


def passed_along(shard, axis, by):
    size = lax.axis_size(axis)
    return lax.ppermute(shard, axis, [(i, (i + by) % size) for i in range(size)])


def broadcast(block, axis, source):
    block = jnp.where(lax.axis_index(axis) == source, block, jnp.zeros_like(block))
    return lax.psum(block, axis)


def contribution(tgt, energy, wav, lvl, perm, vecs, freq, weight):
    cols = jnp.take(wav, perm, axis=1)
    pair = (tgt.astype(jnp.float32)[:, None, :] * cols.astype(jnp.float32)[None, :, :]).astype(
        jnp.bfloat16
    )
    pair = pair.reshape(tgt.shape[0] * wav.shape[0], tgt.shape[1])
    proj = lax.dot_general(pair, vecs, (((1,), (1,)), ((), ())), preferred_element_type=jnp.float32)
    proj = proj.reshape(tgt.shape[0], wav.shape[0], vecs.shape[0])
    gap = energy.astype(jnp.float32)[:, None] - lvl.astype(jnp.float32)[None, :]
    freq32 = freq.astype(jnp.float32)
    factor = (
        weight.astype(jnp.float32) * freq32 / (freq32 * freq32 + gap[:, :, None] * gap[:, :, None])
    )
    return jnp.sum(proj * proj * factor, axis=1)


def forward(packet, moves):
    packet = jax.tree.map(
        lambda part, own: part.astype(own.dtype),
        passed_along(as_sent(packet), "kx", moves[0]),
        packet,
    )
    if moves[1] != 0:
        packet = jax.tree.map(
            lambda part, own: part.astype(own.dtype),
            passed_along(as_sent(packet), "ky", moves[1]),
            packet,
        )
    if moves[2] != 0:
        packet = jax.tree.map(
            lambda part, own: part.astype(own.dtype),
            passed_along(as_sent(packet), "kz", moves[2]),
            packet,
        )
    return packet


def local(
    target,
    target_energy,
    waves,
    band_energy,
    occupation,
    gmap,
    pole_vectors,
    pole_freq,
    pole_weight,
):
    tgt = target[0, 0, 0]
    energy = target_energy[0, 0, 0]
    wav = waves[0, 0, 0]
    level = (band_energy[0, 0, 0] - (2 * occupation[0, 0, 0] - 1).astype(jnp.float32)).astype(
        jnp.bfloat16
    )
    size_y = lax.axis_size("ky")
    size_z = lax.axis_size("kz")
    total = jnp.zeros((tgt.shape[0], pole_vectors.shape[3]), jnp.float32)
    previous = None
    for step, qvec in enumerate(QSTEPS):
        root = qvec[0] * size_y * size_z + qvec[1] * size_z + qvec[2]
        vecs, freq, weight = (
            broadcast(pole_vectors[0, 0, 0], ("kx", "ky", "kz"), root),
            broadcast(pole_freq[0, 0, 0], ("kx", "ky", "kz"), root),
            broadcast(pole_weight[0, 0, 0], ("kx", "ky", "kz"), root),
        )
        perm = gmap[step]
        source = (wav, level)
        previous = forward(source, qvec)
        total = total + contribution(
            tgt, energy, previous[0], previous[1], perm, vecs, freq, weight
        )
    total = total / jnp.float32(wav.shape[0])
    return total[None, None, None]


def solution(mesh):
    return jax.shard_map(
        local,
        mesh=mesh,
        in_specs=(
            P("kx", "ky", "kz", None, None),
            P("kx", "ky", "kz", None),
            P("kx", "ky", "kz", None, None),
            P("kx", "ky", "kz", None),
            P("kx", "ky", "kz", None),
            P(),
            P("kx", "ky", "kz", None, None),
            P("kx", "ky", "kz", None),
            P("kx", "ky", "kz", None),
        ),
        out_specs=P("kx", "ky", "kz", None, None),
        check_vma=False,
    )
```

profile of v0, /device:TPU:1, one launch (start us, length us, event | category | flops | bytes accessed | tf_op | source)
XLA Modules:
  0.0 338.2 jit_solution(10290702199439804394)
XLA Ops:
  6.5 0.0 copy-start.9
  6.5 0.0 all-reduce.4.cloned.1.call-start
  6.5 2.5 copy.10
  9.0 4.8 %collective-permute-start = (bf16[128,4096]{0,1:T(8,128)(2,1)}, bf16[128,4096]{0,1:T(8,128)(2,1)S(1)}, u32[]{:S(2)}, u32[]{:S(2)}) collective-permute-start(bf16[128,4096]{0,1:T(8,128)(2,1)} %bitcast.53), channel_id=1, source_target_pairs={{0,64},{64,128},{128,192},{192,256},{256,320},{320,384},{384,448},... | collective-permute-start | bytes 3145736 | tf_op jit(solution)/shard_map/ppermute | solution.py:15
  13.8 0.0 copy-done.9
  13.8 0.0 copy-done.10
  13.9 4.0 %collective-permute-start.1 = (bf16[128]{0:T(256)(128)(2,1)S(1)}, bf16[128]{0:T(256)(128)(2,1)S(1)}, u32[]{:S(2)}, u32[]{:S(2)}) collective-permute-start(bf16[128]{0:T(256)(128)(2,1)S(1)} %convert_bitcast_fusion), channel_id=1, source_target_pairs={{0,64},{64,128},{128,192},{192,256},{256,320},{320,384},{384,448},... | collective-permute-start | bytes 776 | tf_op jit(solution)/shard_map/ppermute | solution.py:15
  17.9 0.0 copy-done
  17.9 2.8 select_bitcast_fusion.1
  20.7 0.0 copy-start.11
  20.7 0.0 all-reduce.4.cloned.1.call-update
  20.7 0.8 copy-done.4
  21.7 0.0 copy-done.5
  21.7 0.0 copy-done.6
  21.7 111.7 %all-reduce = (bf16[256]{0:T(256)(128)(2,1)S(1)}, bf16[256]{0:T(256)(128)(2,1)S(1)}, bf16[256]{0:T(256)(128)(2,1)S(1)}, bf16[256]{0:T(256)(128)(2,1)S(1)}, bf16[...) all-reduce(bf16[256]{0:T(256)(128)(2,1)S(1)} %get-tuple-element.36,, ...), channel_id=1, replica_groups=mesh['kx'=8,'ky'=8,'kz'=8] {'kx','ky','kz'}, use_global_device_ids=true, to_apply=%region_10.12 | all-reduce | flops 1536 | bytes 6144 | tf_op jit(solution)/shard_map/psum | solution.py:20
  133.5 0.0 copy-done.3
  133.5 0.0 collective-permute-done
  133.5 4.7 %collective-permute-start.2 = (bf16[128,4096]{0,1:T(8,128)(2,1)S(1)}, bf16[128,4096]{0,1:T(8,128)(2,1)S(1)}, u32[]{:S(2)}, u32[]{:S(2)}) collective-permute-start(bf16[128,4096]{0,1:T(8,128)(2,1)S(1)} %collective-permute-done), channel_id=1, source_target_pairs={{0,8},{8,16},{16,24},{24,32},{32,40},{40,48},{48,56},{56,0},{1,9},... | collective-permute-start | bytes 3145736 | tf_op jit(solution)/shard_map/ppermute | solution.py:15
  138.2 0.0 collective-permute-done.1
  138.2 1.9 collective-permute-start.3
  140.2 21.4 %collective-permute-done.3 = bf16[128]{0:T(256)(128)(2,1)S(1)} collective-permute-done((bf16[128]{0:T(256)(128)(2,1)S(1)}, bf16[128]{0:T(256)(128)(2,1)S(1)}, u32[]{:S(2)}, u32[]{:S(2)}) %collective-permute-start.3) | collective-permute-done | bytes 288 | tf_op jit(solution)/shard_map/ppermute | solution.py:15
  161.6 4.1 %collective-permute-start.5 = (bf16[128]{0:T(256)(128)(2,1)S(1)}, bf16[128]{0:T(256)(128)(2,1)S(1)}, u32[]{:S(2)}, u32[]{:S(2)}) collective-permute-start(bf16[128]{0:T(256)(128)(2,1)S(1)} %collective-permute-done.3), channel_id=1, source_target_pairs={{0,1},{1,2},{2,3},{3,4},{4,5},{5,6},{6,7},{7,0},{8,9},{9,10},{10,1... | collective-permute-start | bytes 776 | tf_op jit(solution)/shard_map/ppermute | solution.py:15
  165.6 0.0 copy-done.11
  165.7 2.3 collective-permute-done.5
  167.9 0.1 subtract_multiply_fusion.1
  168.0 12.1 %gather_fusion = bf16[4096,128]{1,0:T(8,128)(2,1)S(1)} fusion(bf16[128,4096]{0,1:T(8,128)(2,1)S(1)} %collective-permute-done, s32[4096]{0:T(1024)S(1)} %fusion.39), kind=kCustom, calls=%fused_computation.clone | custom fusion | bytes 2113536 | tf_op jit(solution)/shard_map/jit(_take)/gather | solution.py:24
  180.2 0.0 collective-permute-done.2
  180.2 2.1 collective-permute-start.4
  182.3 3.2 bitcast_convert_fusion.2
  185.5 2.9 copy.11
  188.4 12.1 %gather_fusion.1 = bf16[4096,128]{1,0:T(8,128)(2,1)S(1)} fusion(bf16[128,4096]{0,1:T(8,128)(2,1)S(1)} %collective-permute-done.2, s32[4096]{0:T(1024)S(1)} %fusion.40), kind=kCustom, calls=%fused_computation.1.clone | custom fusion | bytes 2113536 | tf_op jit(solution)/shard_map/jit(_take)/gather | solution.py:24
  200.5 3.2 bitcast_convert_fusion.1
  203.7 2.9 copy.12
  206.6 0.0 collective-permute-done.4
  206.6 12.1 %gather_fusion.2 = bf16[4096,128]{1,0:T(8,128)(2,1)S(1)} fusion(bf16[128,4096]{0,1:T(8,128)(2,1)S(1)} %collective-permute-done.4, s32[4096]{0:T(1024)S(1)} %fusion.41), kind=kCustom, calls=%fused_computation.2.clone | custom fusion | bytes 2113536 | tf_op jit(solution)/shard_map/jit(_take)/gather | solution.py:24
  218.7 0.7 bitcast_convert_fusion
  219.5 1.9 copy.13
  221.3 99.6 %all-reduce.4.cloned.1.call-done = (bf16[256,4096]{1,0:T(8,128)(2,1)}, bf16[256,4096]{1,0:T(8,128)(2,1)}, bf16[256,4096]{1,0:T(8,128)(2,1)}) async-done(((bf16[256,4096]{1,0:T(8,128)(2,1)}, bf16[256,4096]{1,0:T(8,128)(2,1)}, bf16[256,4096]{1,0:T(8,128)(2,1)}), (bf16[256,4096]{1,0:T(8,128)(2,1)}, bf16[256,4096]{1,0:T(8,128)(2,1)}, bf16[256,4096]{1,0:T(8,128)(2,1)})) %all-reduce.4.cloned.1.call-update) | async-done | bytes 6291472 | tf_op jit(solution)/shard_map/psum | solution.py:20
  321.0 4.8 %fusion.30 = f32[8,256]{1,0:T(8,128)S(1)} fusion(bf16[256,4096]{1,0:T(8,128)(2,1)} %get-tuple-element.18, f32[128,4096]{1,0:T(8,128)} %copy.13, f32[8,4096]{1,0:T(8,128)S(1)} %bitcast_convert_fusion.3, f32[8,128]{1,0:T(8,128)S(1)} %get-tuple-element.30, f32[256]{0:T(256)S(1)} %get-tuple-element.35, f32[256]{0:T(256)S(1)} %get-tuple-element.34), kind=kOutput, calls=%fused_computation.27 | convolution fusion | flops 2157180928 | bytes 4339712 | tf_op jit(solution)/shard_map/dot_general | solution.py:29
  325.8 0.0 copy-done.2
  325.8 0.0 copy-done.8
  325.8 0.0 copy-start.1
  325.8 0.0 copy-start.7
  325.8 2.4 fusion.36
  328.2 0.0 copy-done.1
  328.3 0.0 copy-done.7
  328.3 2.5 fusion.33
  330.7 0.6 multiply_bitcast_fusion
  (25 shorter events, 0.2 us)
Async XLA Ops:
  6.5 7.3 %copy-start.9 = (f32[1,1,1,128]{3,2,1,0:T(1,128)S(1)}, f32[1,1,1,128]{3,2,1,0:T(1,128)}, u32[]{:S(2)}) copy-start(f32[1,1,1,128]{3,2,1,0:T(1,128)} %param.14) | copy-start | bytes 1540
  6.5 7.3 %copy-start.10 = (s32[1,1,1,128]{3,2,1,0:T(1,128)S(1)}, s32[1,1,1,128]{3,2,1,0:T(1,128)}, u32[]{:S(2)}) copy-start(s32[1,1,1,128]{3,2,1,0:T(1,128)} %param.15) | copy-start | bytes 1540
  6.5 11.4 %copy-start = (bf16[1,1,1,256,4096]{4,3,2,1,0:T(8,128)(2,1)S(1)}, bf16[1,1,1,256,4096]{4,3,2,1,0:T(8,128)(2,1)}, u32[]{:S(2)}) copy-start(bf16[1,1,1,256,4096]{4,3,2,1,0:T(8,128)(2,1)} %param.17) | copy-start | bytes 6291460
  6.5 314.4 %all-reduce.4.cloned.1.call-start = ((), (), s32[]{:S(2)}) async-start(), calls=%async_computation | async-start | bytes 12582912 | tf_op jit(solution)/shard_map/psum | solution.py:20
  9.0 124.5 %collective-permute-start = (bf16[128,4096]{0,1:T(8,128)(2,1)}, bf16[128,4096]{0,1:T(8,128)(2,1)S(1)}, u32[]{:S(2)}, u32[]{:S(2)}) collective-permute-start(bf16[128,4096]{0,1:T(8,128)(2,1)} %bitcast.53), channel_id=1, source_target_pairs={{0,64},{64,128},{128,192},{192,256},{256,320},{320,384},{384,448},... | collective-permute-start | bytes 3145736 | tf_op jit(solution)/shard_map/ppermute | solution.py:15
  13.9 124.3 %collective-permute-start.1 = (bf16[128]{0:T(256)(128)(2,1)S(1)}, bf16[128]{0:T(256)(128)(2,1)S(1)}, u32[]{:S(2)}, u32[]{:S(2)}) collective-permute-start(bf16[128]{0:T(256)(128)(2,1)S(1)} %convert_bitcast_fusion), channel_id=1, source_target_pairs={{0,64},{64,128},{128,192},{192,256},{256,320},{320,384},{384,448},... | collective-permute-start | bytes 776 | tf_op jit(solution)/shard_map/ppermute | solution.py:15
  20.7 0.8 copy-start.4
  20.7 1.0 copy-start.5
  20.7 1.0 copy-start.6
  20.7 112.8 %copy-start.3 = (bf16[1,1,1,8,4096]{4,3,2,1,0:T(8,128)(2,1)S(1)}, bf16[1,1,1,8,4096]{4,3,2,1,0:T(8,128)(2,1)}, u32[]{:S(2)}) copy-start(bf16[1,1,1,8,4096]{4,3,2,1,0:T(8,128)(2,1)} %param.11) | copy-start | bytes 196612
  20.7 144.9 %copy-start.11 = (bf16[1,1,1,8]{3,2,1,0:T(2,128)(2,1)S(1)}, bf16[1,1,1,8]{3,2,1,0:T(2,128)(2,1)}, u32[]{:S(2)}) copy-start(bf16[1,1,1,8]{3,2,1,0:T(2,128)(2,1)} %param.12) | copy-start | bytes 52
  133.5 46.7 %collective-permute-start.2 = (bf16[128,4096]{0,1:T(8,128)(2,1)S(1)}, bf16[128,4096]{0,1:T(8,128)(2,1)S(1)}, u32[]{:S(2)}, u32[]{:S(2)}) collective-permute-start(bf16[128,4096]{0,1:T(8,128)(2,1)S(1)} %collective-permute-done), channel_id=1, source_target_pairs={{0,8},{8,16},{16,24},{24,32},{32,40},{40,48},{48,56},{56,0},{1,9},... | collective-permute-start | bytes 3145736 | tf_op jit(solution)/shard_map/ppermute | solution.py:15
  138.2 23.3 %collective-permute-start.3 = (bf16[128]{0:T(256)(128)(2,1)S(1)}, bf16[128]{0:T(256)(128)(2,1)S(1)}, u32[]{:S(2)}, u32[]{:S(2)}) collective-permute-start(bf16[128]{0:T(256)(128)(2,1)S(1)} %collective-permute-done.1), channel_id=1, source_target_pairs={{0,8},{8,16},{16,24},{24,32},{32,40},{40,48},{48,56},{56,0},{1,9},... | collective-permute-start | bytes 776 | tf_op jit(solution)/shard_map/ppermute | solution.py:15
  161.6 6.4 %collective-permute-start.5 = (bf16[128]{0:T(256)(128)(2,1)S(1)}, bf16[128]{0:T(256)(128)(2,1)S(1)}, u32[]{:S(2)}, u32[]{:S(2)}) collective-permute-start(bf16[128]{0:T(256)(128)(2,1)S(1)} %collective-permute-done.3), channel_id=1, source_target_pairs={{0,1},{1,2},{2,3},{3,4},{4,5},{5,6},{6,7},{7,0},{8,9},{9,10},{10,1... | collective-permute-start | bytes 776 | tf_op jit(solution)/shard_map/ppermute | solution.py:15
  180.2 26.4 %collective-permute-start.4 = (bf16[128,4096]{0,1:T(8,128)(2,1)S(1)}, bf16[128,4096]{0,1:T(8,128)(2,1)S(1)}, u32[]{:S(2)}, u32[]{:S(2)}) collective-permute-start(bf16[128,4096]{0,1:T(8,128)(2,1)S(1)} %collective-permute-done.2), channel_id=1, source_target_pairs={{0,1},{1,2},{2,3},{3,4},{4,5},{5,6},{6,7},{7,0},{8,9},{9,10},{10,1... | collective-permute-start | bytes 3145736 | tf_op jit(solution)/shard_map/ppermute | solution.py:15
  321.0 4.8 %copy-start.2 = (f32[128,4096]{1,0:T(8,128)S(1)}, f32[128,4096]{1,0:T(8,128)}, u32[]{:S(2)}) copy-start(f32[128,4096]{1,0:T(8,128)} %copy.11) | copy-start | bytes 6291460
  321.0 4.8 %copy-start.8 = (bf16[256,4096]{1,0:T(8,128)(2,1)S(1)}, bf16[256,4096]{1,0:T(8,128)(2,1)}, u32[]{:S(2)}) copy-start(bf16[256,4096]{1,0:T(8,128)(2,1)} %get-tuple-element.19) | copy-start | bytes 6291460
  325.8 2.5 copy-start.1
  325.8 2.5 copy-start.7
Sparse Core Ops, SparseCore 0:
  20.9 300.0 all-reduce.3
where the time goes:
time: 339 us; the launch traced here: 338 us
  waiting for transfers between devices  123 us (36%)
  blocking collectives  112 us (33%)
  local copies, waits for them, and re-layouts  47.4 us (14%)
  starting transfers between devices  21.6 us (6%)
  between operations  13.8 us (4%)
  other arithmetic  10.7 us (3%)
  matrix products  9.68 us (3%)
    psum x1, blocking collectives, broadcast(): return lax.psum(block, axis)  112 us
    psum x1, waiting for transfers between devices, broadcast(): return lax.psum(block, axis)  99.6 us
    gather x3, local copies, waits for them, and re-layouts, contribution(): cols = jnp.take(wav, perm, axis=1)  36.4 us
    ppermute x6, waiting for transfers between devices, passed_along(): lax.ppermute(shard, axis, [(i, (i + by) % size) for i in range(size)])  23.7 us
    ppermute x6, starting transfers between devices, passed_along(): lax.ppermute(shard, axis, [(i, (i + by) % size) for i in range(size)])  21.6 us
    dot_general x3, matrix products, contribution(): lax.dot_general(pair, vecs, (((1,), (1,)), ((), ())), preferred_element_t...  9.68 us
    convert_element_type x3, local copies, waits for them, and re-layouts, contribution(): cols.astype(jnp.float32)[None, :, :]  7.67 us
    convert_element_type x3, other arithmetic, contribution(): cols.astype(jnp.float32)[None, :, :]  7.05 us
  transfers between devices with their start and end apart: 7, of which 3 were waited for; matrix products, arithmetic and copies ran while one was open for 16% of the time, Pallas kernels for 0%

commit v1 on v0

v1 whole, which is shorter than its diff:
```python
import functools

import jax
import jax.numpy as jnp
from jax import lax
from jax.experimental import pallas as pl
from jax.experimental.pallas import tpu as pltpu
from jax.sharding import PartitionSpec as P

MESH = pl.DeviceIdType.MESH
QSTEPS = ((1, 0, 0), (1, 1, 0), (1, 1, 1))
NQ = 3
BLK = 256
SUB = 4
ROWS = BLK // SUB
EXTRA = 16
NEAR = {1: (0, 1, 0), 2: (1, 0, 0), 3: (0, 0, 1), 5: (0, 0, -1), 6: (-1, 0, 0), 7: (0, -1, 0)}
FAR = ((2, 0, 0), (0, 1, 1), (0, -1, -1))
WAY = [[FAR[s] if t == 4 else NEAR[t] for s in range(NQ)] for t in range(1, 8)]


def chip_of(me):
    kx, ky, kz = me
    return kz % 4, (ky // 2) * 2 + kz // 4, kx, ky % 2


def device_of(x, y, z, c):
    return z, (y // 2) * 2 + c, (y % 2) * 4 + x


def kernel(
    gmap, vecs, waves, target, energy_row, band_energy, occupation, freq_row, weight_row, out,
    held, made, onehot, own, sent, tgt, moved, total, factor, answer, part, level, pole,
    own_sem, ss1, ss2, ss3, ss4, sst, ssr, rs2, rs3, rs4, rst, rsr,
):
    me = tuple(lax.axis_index(a) for a in ("kx", "ky", "kz"))
    x, y, z, c = chip_of(me)
    cls = (2 * x + y + 3 * z) % 8
    mine = cls + 8 * c

    def chip(dx, dy, dz, core=c):
        return device_of((x + dx + 4) % 4, (y + dy + 8) % 8, (z + dz + 8) % 8, core)

    def shifted(q, sign):
        return tuple((i + sign * d + 8) % 8 for i, d in zip(me, q))

    sibling = chip(0, 0, 0, 1 - c)
    is_source = (z == 1) & (y == 0) & ((x == 0) | ((x == 1) & (c == 1)))
    source_q = jnp.where(x == 0, c, 2)
    held_q = ((z + 8 - 4 * c) % 8) // 3
    is_holder = (z + 8 - 4 * c) % 8 == 3 * held_q

    barrier = pltpu.get_barrier_semaphore()

    def hello(device):
        pl.semaphore_signal(barrier, inc=1, device_id=device, device_id_type=MESH)

    for q in QSTEPS:
        hello(shifted(q, 1))
        hello(shifted(q, -1))
    hello(sibling)
    for t in range(7):
        for way in sorted(set(WAY[t])):
            hello(chip(-way[0], -way[1], -way[2]))

    def greet(i, _):
        s, hx = i // 4, i % 4
        hz = (3 * s + 4 * c) % 8
        hy = (cls + 48 - 2 * hx - 3 * hz) % 8

        @pl.when(jnp.logical_not((hx == x) & (hz == z)))
        def _():
            hello(device_of(hx, hy, hz, c))

        return 0

    lax.fori_loop(0, NQ * SUB, greet, 0)

    @pl.when(is_holder)
    def _():
        hello(device_of(jnp.where(held_q == 2, 1, 0), 0, 1, jnp.where(held_q == 0, 0, 1)))

    load = pltpu.make_async_copy(vecs, own, own_sem)

    @pl.when(is_source)
    def _():
        load.start()

    def wanted(q):
        row = gmap[pl.ds(q, 1), :]
        return row // BLK, row % BLK

    def fill_onehot(low):
        for r in range(0, BLK, 32):
            rows = lax.broadcasted_iota(jnp.int32, (32, low.shape[1]), 0) + r
            onehot[r : r + 32, :] = jnp.where(rows == low, 1.0, 0.0).astype(jnp.bfloat16)

    sent[:, : target.shape[1]] = target[...].astype(jnp.float32)
    spot = lax.broadcasted_iota(jnp.int32, (8, 8), 0) == lax.broadcasted_iota(jnp.int32, (8, 8), 1)
    spot = jnp.where(spot, jnp.broadcast_to(energy_row[...].astype(jnp.float32), (8, 8)), 0.0)
    sent[:, target.shape[1] :] = jnp.broadcast_to(jnp.sum(spot, axis=1, keepdims=True), (8, 128))
    lvl_row = band_energy[...] - (2 * occupation[...] - 1).astype(jnp.float32)
    lvl_row = lvl_row.astype(jnp.bfloat16).astype(jnp.float32)
    level[...] = jnp.broadcast_to(lvl_row, (128, 128)).T
    row_at = lax.broadcasted_iota(jnp.int32, (EXTRA, 256), 0)
    pole[...] = jnp.where(
        row_at == 0,
        freq_row[...].astype(jnp.float32),
        jnp.where(row_at == 1, weight_row[...].astype(jnp.float32), 0.0),
    ).astype(jnp.bfloat16)

    peers = 2 * NQ + 1 + 9
    pl.semaphore_wait(barrier, peers + jnp.where(is_holder, 31, 0) + jnp.where(is_source, 16 * SUB, 0))

    def target_copy(s):
        return pltpu.make_async_remote_copy(
            sent, tgt.at[s], sst.at[s], rst.at[s], device_id=shifted(QSTEPS[s], -1), device_id_type=MESH
        )

    @pl.when(is_source)
    def _():
        load.wait()
        high, low = wanted(source_q)
        fill_onehot(low)

        def hand_out(pos, _):
            j = pos // 2 + 8 * (pos % 2)
            dest_c = pos % 2
            dest_cls = pos // 2
            mask = jnp.where(high == j, 1.0, 0.0).astype(jnp.bfloat16)
            block = lax.dot_general(
                onehot[...], own[...] * mask, (((1,), (1,)), ((), ())), preferred_element_type=jnp.float32
            )
            made[j, :BLK, :] = block.astype(jnp.bfloat16)
            made[j, BLK:, :] = pole[...]
            hz = (3 * source_q + 4 * dest_c) % 8
            for u in range(SUB):
                hy = (dest_cls + 48 - 2 * u - 3 * hz) % 8
                rows = pl.ds(u * ROWS, ROWS + (EXTRA if u == SUB - 1 else 0))
                pltpu.make_async_remote_copy(
                    made.at[j, rows], held.at[source_q, j, rows], ss1.at[j, u], rs2.at[source_q, u],
                    device_id=device_of(u, hy, hz, dest_c), device_id_type=MESH,
                ).start()
            return 0

        lax.fori_loop(0, 16, hand_out, 0)

    for s in range(NQ):
        target_copy(s).start()

    def permute_target(s, _):
        high, low = wanted(s)
        fill_onehot(low)
        pltpu.make_async_remote_copy(
            sent, tgt.at[s], sst.at[s], rst.at[s], device_id=sibling, device_id_type=MESH
        ).wait_recv()
        t = tgt[s, :, : target.shape[1]]
        rows = jnp.concatenate([jnp.where(high == j, t, 0.0).astype(jnp.bfloat16) for j in range(16)], axis=0)
        ordered = lax.dot_general(
            rows, onehot[...], (((1,), (1,)), ((), ())), preferred_element_type=jnp.float32
        )
        for j in range(16):
            moved[s, j] = ordered[8 * j : 8 * j + 8, :]
        return 0

    lax.fori_loop(0, NQ, permute_target, 0)

    def part_copy(s, u, slot, device):
        n = ROWS + (EXTRA if u == SUB - 1 else 0)
        rows = pl.ds(u * ROWS, n)
        return pltpu.make_async_remote_copy(
            held.at[s, mine, rows], held.at[s, mine, rows], ss2.at[slot], rs2.at[s, u],
            device_id=device, device_id_type=MESH,
        )

    @pl.when(is_holder)
    def _():
        for u in range(SUB):

            @pl.when(x == u)
            def _():
                part_copy(held_q, u, 0, sibling).wait_recv()

                def give(i, _):
                    dx, dz = (i + 1) % 4, (i + 1) // 4
                    dy = (64 - 2 * dx - 3 * dz) % 8
                    part_copy(held_q, u, i, chip(dx, dy, dz)).start()
                    return 0

                lax.fori_loop(0, 31, give, 0)

    total[...] = jnp.zeros_like(total)

    def near_copy(s, t):
        return pltpu.make_async_remote_copy(
            held.at[s, mine, pl.ds(0, BLK)], held.at[s, mine, pl.ds(0, BLK)], ss3.at[s, t], rs3.at[s, cls],
            device_id=chip(*WAY[t][s]), device_id_type=MESH,
        )

    def chunk_in(s, k, sem):
        j = k + 8 * c
        return pltpu.make_async_remote_copy(
            held.at[s, j, pl.ds(0, BLK)], held.at[s, j, pl.ds(0, BLK)], ss3.at[0, 0], sem,
            device_id=sibling, device_id_type=MESH,
        )

    def side_copy(s, k):
        j = k + 8 * c
        return pltpu.make_async_remote_copy(
            held.at[s, j, pl.ds(0, BLK)], held.at[s, j, pl.ds(0, BLK)], ss4.at[s, k], rs4.at[s, k],
            device_id=sibling, device_id_type=MESH,
        )

    def side_in(s, k):
        j = k + 8 * (1 - c)
        return pltpu.make_async_remote_copy(
            held.at[s, j, pl.ds(0, BLK)], held.at[s, j, pl.ds(0, BLK)], ss4.at[s, k], rs4.at[s, k],
            device_id=sibling, device_id_type=MESH,
        )

    def spread(s):
        for u in range(SUB):

            @pl.when(jnp.logical_not(is_holder & (held_q == s) & (x == u)))
            def _():
                part_copy(s, u, 0, sibling).wait_recv()

        for t in range(7):
            near_copy(s, t).start()

    def make_factor(s):
        freq = held[s, mine, BLK : BLK + EXTRA, :].astype(jnp.float32)
        f, w = freq[0:1, :], freq[1:2, :]
        wf, ff = w * f, f * f
        e = tgt[s, :, target.shape[1] :]
        lvl = level[...]
        for m in range(8):
            gap = e[m : m + 1, :] - lvl
            gap = gap * gap
            gap = jnp.concatenate([gap, gap], axis=1)
            factor[s, m * 128 : m * 128 + 128, :] = wf / (ff + gap)

    def work(s, j):
        w = waves[:, pl.ds(pl.multiple_of(j * BLK, BLK), BLK)].astype(jnp.float32)
        t = moved[s, j]
        pair = jnp.concatenate([(t[m : m + 1, :] * w).astype(jnp.bfloat16) for m in range(8)], axis=0)
        total[s] += jnp.dot(pair, held[s, j, :BLK, :], preferred_element_type=jnp.float32)

    due = jnp.maximum(cls - 4, 0)

    def turn(k, _):
        @pl.when(k == due)
        def _():
            for s in range(NQ):
                spread(s)
            for s in range(NQ):
                make_factor(s)

        def arrive(s, _):
            @pl.when(k != cls)
            def _():
                chunk_in(s, k, rs3.at[s, k]).wait_recv()

            side_copy(s, k).start()
            work(s, k + 8 * c)
            return 0

        lax.fori_loop(0, NQ, arrive, 0)

        def arrive_side(s, _):
            side_in(s, k).wait_recv()
            work(s, k + 8 * (1 - c))
            return 0

        lax.fori_loop(0, NQ, arrive_side, 0)
        return 0

    lax.fori_loop(0, 8, turn, 0)

    def answer_copy(s):
        return pltpu.make_async_remote_copy(
            answer.at[s], part.at[s], ssr.at[s], rsr.at[s], device_id=shifted(QSTEPS[s], 1), device_id_type=MESH
        )

    for s in range(NQ):
        for m in range(8):
            rows = slice(m * 128, m * 128 + 128)
            proj = total[s, rows, :]
            answer[s, m : m + 1, :] = jnp.sum(proj * proj * factor[s, rows, :], axis=0, keepdims=True)
        answer_copy(s).start()

    for s in range(NQ):
        target_copy(s).wait_send()
        for t in range(7):
            near_copy(s, t).wait_send()

    def side_left(k, _):
        for s in range(NQ):
            side_copy(s, k).wait_send()
        return 0

    lax.fori_loop(0, 8, side_left, 0)

    @pl.when(is_holder)
    def _():
        for u in range(SUB):

            @pl.when(x == u)
            def _():
                def left(i, _):
                    part_copy(held_q, u, i, sibling).wait_send()
                    return 0

                lax.fori_loop(0, 31, left, 0)

    @pl.when(is_source)
    def _():
        def left(j, _):
            for u in range(SUB):
                rows = pl.ds(u * ROWS, ROWS + (EXTRA if u == SUB - 1 else 0))
                pltpu.make_async_remote_copy(
                    made.at[j, rows], held.at[source_q, j, rows], ss1.at[j, u], rs2.at[source_q, u],
                    device_id=sibling, device_id_type=MESH,
                ).wait_send()
            return 0

        lax.fori_loop(0, 16, left, 0)

    for s in range(NQ):
        answer_copy(s).wait()
    out[...] = (part[0] + part[1] + part[2]) * (1.0 / 128.0)


def local(target, target_energy, waves, band_energy, occupation, gmap, pole_vectors, pole_freq, pole_weight):
    tgt = target[0, 0, 0]
    vmem = pl.BlockSpec(memory_space=pltpu.VMEM)
    dma = pltpu.SemaphoreType.DMA
    out = pl.pallas_call(
        kernel,
        out_shape=jax.ShapeDtypeStruct((8, 256), jnp.float32),
        in_specs=[vmem, pl.BlockSpec(memory_space=pl.ANY)] + [vmem] * 7,
        out_specs=vmem,
        scratch_shapes=[
            pltpu.VMEM((NQ, 16, BLK + EXTRA, 256), jnp.bfloat16),
            pltpu.VMEM((16, BLK + EXTRA, 256), jnp.bfloat16),
            pltpu.VMEM((BLK, 4096), jnp.bfloat16),
            pltpu.VMEM((256, 4096), jnp.bfloat16),
            pltpu.VMEM((8, 4096 + 128), jnp.float32),
            pltpu.VMEM((NQ, 8, 4096 + 128), jnp.float32),
            pltpu.VMEM((NQ, 16, 8, BLK), jnp.float32),
            pltpu.VMEM((NQ, 1024, 256), jnp.float32),
            pltpu.VMEM((NQ, 1024, 256), jnp.float32),
            pltpu.VMEM((NQ, 8, 256), jnp.float32),
            pltpu.VMEM((NQ, 8, 256), jnp.float32),
            pltpu.VMEM((128, 128), jnp.float32),
            pltpu.VMEM((EXTRA, 256), jnp.bfloat16),
            dma,
            dma((16, SUB)),
            dma((31,)),
            dma((NQ, 7)),
            dma((NQ, 8)),
            dma((NQ,)),
            dma((NQ,)),
            dma((NQ, SUB)),
            dma((NQ, 8)),
            dma((NQ, 8)),
            dma((NQ,)),
            dma((NQ,)),
        ],
        compiler_params=pltpu.CompilerParams(
            collective_id=0, has_side_effects=True, vmem_limit_bytes=56 << 20
        ),
    )(
        gmap, pole_vectors[0, 0, 0], waves[0, 0, 0], tgt, target_energy[0, 0], band_energy[0, 0],
        occupation[0, 0], pole_freq[0, 0], pole_weight[0, 0],
    )
    return out[None, None, None]


def solution(mesh):
    cut = P("kx", "ky", "kz", None, None)
    row = P("kx", "ky", "kz", None)
    return jax.shard_map(
        local,
        mesh=mesh,
        in_specs=(cut, row, cut, row, row, P(), cut, row, row),
        out_specs=cut,
        check_vma=False,
    )
```

time: 339 us -> 97.9 us (0.29)
  waiting for transfers between devices: 123 us -> 0 us
  blocking collectives: 112 us -> 0 us
  Pallas kernels: 0 us -> 96.4 us
  local copies, waits for them, and re-layouts: 47.4 us -> 1.3 us
  starting transfers between devices: 21.6 us -> 0 us
  between operations: 13.8 us -> 0.01 us
  other arithmetic: 10.7 us -> 0 us
  matrix products: 9.68 us -> 0 us
    psum x1 -> x0, blocking collectives: 112 us -> none  [broadcast(): return lax.psum(block, axis)]
    psum x1 -> x0, waiting for transfers between devices: 99.6 us -> none  [broadcast(): return lax.psum(block, axis)]
    pallas_call x0 -> x1, Pallas kernels: none -> 96.4 us  [local(): pl.pallas_call(kernel, out_shape=jax.ShapeDtypeStruct((8, 256), jnp.float...]
    gather x3 -> x0, local copies, waits for them, and re-layouts: 36.4 us -> none  [contribution(): cols = jnp.take(wav, perm, axis=1)]
    ppermute x6 -> x0, waiting for transfers between devices: 23.7 us -> none  [passed_along(): lax.ppermute(shard, axis, [(i, (i + by) % size) for i in range(size)])]
    ppermute x6 -> x0, starting transfers between devices: 21.6 us -> none  [passed_along(): lax.ppermute(shard, axis, [(i, (i + by) % size) for i in range(size)])]
    dot_general x3 -> x0, matrix products: 9.68 us -> none  [contribution(): lax.dot_general(pair, vecs, (((1,), (1,)), ((), ())), preferred_element_t...]
    convert_element_type x3 -> x0, local copies, waits for them, and re-layouts: 7.67 us -> none  [contribution(): cols.astype(jnp.float32)[None, :, :]]
  transfers between devices with their start and end apart: 7 -> 0, of which waited for: 3 -> 0; matrix products, arithmetic and copies ran while one was open for 16% -> 0% of each run, Pallas kernels for 0% -> 0%
where the time goes in v1:
time: 97.9 us; the launch traced here: 97.7 us
  Pallas kernels  96.4 us (98%)
  local copies, waits for them, and re-layouts  1.3 us (1%)
    pallas_call x1, Pallas kernels, local(): pl.pallas_call(kernel, out_shape=jax.ShapeDtypeStruct((8, 256), jnp.float...  96.4 us

profile of v1, /device:TPU:1, one launch (start us, length us, event | category | flops | bytes accessed | tf_op | source)
XLA Modules:
  0.0 97.7 jit_solution(8170321303739890157)
XLA Ops:
  0.0 96.4 %shard_map.91 = f32[8,256]{1,0:T(8,128)} custom-call(s32[3,4096]{1,0:T(4,128)} %gmap.1, bf16[256,4096]{1,0:T(8,128)(2,1)} %bitcast.9, bf16[128,4096]{1,0:T(8,128)(2,1)} %bitcast.10, bf16[8,4096]{1,0:T(8,128)(2,1)} %bitcast.11, bf16[1,8]{1,0:T(2,128)(2,1)} %bitcast.15, f32[1,128]{1,0:T(1,128)} %bitcast.16, s32[1,128]{1,0:T(1,128)} %bitcast.17, ...), custom_call_target="tpu_custom_call" | custom-call | tf_op jit(solution)/shard_map/pallas_call | solution.py:338
  96.4 1.3 %copy.11 = f32[1,1,1,8,256]{4,3,2,1,0:T(8,128)} copy(f32[1,1,1,8,256]{4,3,2,1,0:T(8,128)} %bitcast.12) | data formatting | bytes 16384

commit v2 on v1

v2 whole, which is shorter than its diff:
```python
import functools

import jax
import jax.numpy as jnp
from jax import lax
from jax.experimental import pallas as pl
from jax.experimental.pallas import tpu as pltpu
from jax.sharding import PartitionSpec as P

MESH = pl.DeviceIdType.MESH
QSTEPS = ((1, 0, 0), (1, 1, 0), (1, 1, 1))
NQ = 3
BLK = 256
SUB = 4
ROWS = BLK // SUB
AHEAD = 8
EXTRA = 16
NEAR = {1: (0, 1, 0), 2: (1, 0, 0), 3: (0, 0, 1), 5: (0, 0, -1), 6: (-1, 0, 0), 7: (0, -1, 0)}
FAR = ((2, 0, 0), (0, 1, 1), (0, -1, -1))
WAY = [[FAR[s] if t == 4 else NEAR[t] for s in range(NQ)] for t in range(1, 8)]


def chip_of(me):
    kx, ky, kz = me
    return kz % 4, (ky // 2) * 2 + kz // 4, kx, ky % 2


def device_of(x, y, z, c):
    return z, (y // 2) * 2 + c, (y % 2) * 4 + x


def kernel(
    gmap, vecs, waves, target, energy_row, band_energy, occupation, freq_row, weight_row, out,
    held, made, onehot, own, sent, tgt, moved, total, factor, answer, part, level, pole,
    own_sem, ss1, ss2, ss3, ss4, sst, ssr, rs1, rs2, rs3, rs4, rst, rsr, ready,
):
    me = tuple(lax.axis_index(a) for a in ("kx", "ky", "kz"))
    x, y, z, c = chip_of(me)
    cls = (2 * x + y + 3 * z) % 8
    mine = cls + 8 * c

    def chip(dx, dy, dz, core=c):
        return device_of((x + dx + 4) % 4, (y + dy + 8) % 8, (z + dz + 8) % 8, core)

    def shifted(q, sign):
        return tuple((i + sign * d + 8) % 8 for i, d in zip(me, q))

    sibling = chip(0, 0, 0, 1 - c)
    is_source = (z == 1) & (y == 0) & ((x == 0) | ((x == 1) & (c == 1)))
    source_q = jnp.where(x == 0, c, 2)
    late = z >= 4
    early = jnp.logical_not(late)
    held_at = (z + 7 - 4 * c) % 8
    held_q = jnp.minimum(held_at // 2, 2)
    is_holder = (held_at == 0) | (held_at == 2) | (held_at == 5)
    relay_no = jnp.where(z == 2, 3 - c, jnp.where(x == 3, 0, 1))
    is_relay = (y == 0) & (((x == 0) & (z == 2)) | ((z == 1) & (((x == 3) & (c == 1)) | ((x == 1) & (c == 0)))))
    gives = (is_source & (source_q != 1)) | is_relay

    def first_z(s, core):
        return (1 + 2 * s + s // 2 + 4 * core) % 8

    def relay_of(k):
        r = k // 2
        return device_of(
            jnp.where(r == 0, 3, jnp.where(r == 1, 1, 0)),
            0,
            jnp.where(r < 2, 1, 2),
            jnp.where((r == 0) | (r == 2), 1, 0),
        )

    def source_of(s):
        return device_of(jnp.where(s == 2, 1, 0), 0, 1, jnp.where(s == 0, 0, 1))

    def holder_of(s, u, k, core):
        hz = first_z(s, core)
        return u, (k + 48 - 2 * u - 3 * hz) % 8, hz

    def giver_of_mine():
        to_relay = held_q == 1
        return tuple(jnp.where(to_relay, a, b) for a, b in zip(relay_of(cls), source_of(held_q)))

    barrier = pltpu.get_barrier_semaphore()

    def hello(device):
        pl.semaphore_signal(barrier, inc=1, device_id=device, device_id_type=MESH)

    def say_ready(device):
        pl.semaphore_signal(ready, inc=1, device_id=device, device_id_type=MESH)

    pairs = [(shifted(q, -1), shifted(q, 1), -1) for q in QSTEPS]
    pairs += [(shifted(q, 1), shifted(q, -1), 1) for q in QSTEPS]
    pairs.append((sibling, sibling, 0))
    for t in range(7):
        for w in sorted(set(WAY[t])):
            pairs.append((chip(*w), chip(-w[0], -w[1], -w[2]), w[2]))
    for to, back, dz in pairs:
        if dz == 0:
            hello(back)
        else:
            first, last = (3, 4) if dz > 0 else (0, 7)

            @pl.when(z != last)
            def _():
                hello(back)

            @pl.when(z == first)
            def _():
                hello(to)

    def holder_of_mine(i):
        u, hy, hz = holder_of(i // 4, i % 4, cls, c)
        return device_of(u, hy, hz, c), (u == x) & (hz == z), hz >= 4

    def greet(i, _):
        device, own_place, is_late = holder_of_mine(i)

        @pl.when(jnp.logical_not(own_place) & (early | is_late))
        def _():
            hello(device)

        return 0

    def peer(i, base):
        px, pz = (x + i) % 4, base + (z + i // 4) % 4
        return device_of(px, (cls + 48 - 2 * px - 3 * pz) % 8, pz, c)

    lax.fori_loop(0, NQ * SUB, greet, 0)

    @pl.when(is_holder & early)
    def _():
        @pl.when(jnp.logical_not(is_source & (source_q == 0)))
        def _():
            hello(giver_of_mine())

        def greet_late(i, _):
            hello(peer(i, 4))
            return 0

        lax.fori_loop(0, 16, greet_late, 0)

    @pl.when(is_relay)
    def _():
        hello(source_of(1))

    def given_to(i):
        q = jnp.where(is_relay, 1, source_q)
        core = jnp.where(q == 2, 0, 1)
        k = jnp.where(is_relay, 2 * relay_no, 0) + i // 4
        u, hy, hz = holder_of(q, i % 4, k, core)
        return device_of(u, hy, hz, core)

    many = jnp.where(is_relay, 8, 32)

    @pl.when(gives)
    def _():
        def greet_given(i, _):
            hello(given_to(i))
            return 0

        lax.fori_loop(0, many, greet_given, 0)

    load = pltpu.make_async_copy(vecs, own, own_sem)

    @pl.when(is_source)
    def _():
        load.start()

    def wanted(q):
        row = gmap[pl.ds(q, 1), :]
        return row // BLK, row % BLK

    def fill_onehot(low):
        for r in range(0, BLK, 32):
            rows = lax.broadcasted_iota(jnp.int32, (32, low.shape[1]), 0) + r
            onehot[r : r + 32, :] = jnp.where(rows == low, 1.0, 0.0).astype(jnp.bfloat16)

    half = target.shape[1] // 2
    for h in range(2):
        sent[8 * h : 8 * h + 8, :half] = target[:, h * half : h * half + half].astype(jnp.float32).astype(jnp.bfloat16)
    spot = lax.broadcasted_iota(jnp.int32, (8, 8), 0) == lax.broadcasted_iota(jnp.int32, (8, 8), 1)
    spot = jnp.where(spot, jnp.broadcast_to(energy_row[...].astype(jnp.float32), (8, 8)), 0.0)
    spot = jnp.broadcast_to(jnp.sum(spot, axis=1, keepdims=True), (8, 128))
    sent[:, half:] = jnp.concatenate([spot, spot], axis=0).astype(jnp.bfloat16)
    lvl_row = band_energy[...] - (2 * occupation[...] - 1).astype(jnp.float32)
    lvl_row = lvl_row.astype(jnp.bfloat16).astype(jnp.float32)
    level[...] = jnp.broadcast_to(lvl_row, (128, 128)).T
    row_at = lax.broadcasted_iota(jnp.int32, (EXTRA, 256), 0)
    pole[...] = jnp.where(
        row_at == 0,
        freq_row[...].astype(jnp.float32),
        jnp.where(row_at == 1, weight_row[...].astype(jnp.float32), 0.0),
    ).astype(jnp.bfloat16)

    edge = (z == 0) | (z == 3)
    peers = 2 * NQ + 1 + 9
    first_held = jnp.where(c == 0, 8, 4)
    greeted_early = (
        peers
        - jnp.where(edge, 5, 0)
        + jnp.where(is_holder, 15, 0)
        + jnp.where(is_relay, 8, 0)
        + jnp.where(is_source, jnp.where(source_q == 0, 31, jnp.where(source_q == 1, 4, 32)), 0)
    )
    greeted_late = (
        peers
        + jnp.where((z == 4) | (z == 7), 5, 0)
        + first_held
        + jnp.where(is_holder, 32, 0)
    )
    greeted = jnp.where(late, greeted_late, greeted_early)
    answers = jnp.where(edge, 5, 0) + jnp.where(is_holder, 16, 0) + jnp.where(gives, many, 0)

    def target_copy(s):
        return pltpu.make_async_remote_copy(
            sent, tgt.at[s], sst.at[s], rst.at[s], device_id=shifted(QSTEPS[s], -1), device_id_type=MESH
        )

    def part_rows(u):
        return pl.ds(u * ROWS, ROWS + (EXTRA if u == SUB - 1 else 0))

    def hand_copy(q, j, u):
        core = j // 8
        hx, hy, hz = holder_of(q, u, j % 8, core)
        own_place = (hx == x) & (hy == y) & (hz == z) & (core == c)
        rows = part_rows(u)
        copy = pltpu.make_async_remote_copy(
            made.at[j, rows], held.at[q, j, rows], ss1.at[j, u], rs2.at[q, u],
            device_id=device_of(hx, hy, hz, core), device_id_type=MESH,
        )
        return copy, own_place, rows

    def hand_out(q, j):
        for u in range(SUB):
            copy, own_place, rows = hand_copy(q, j, u)

            @pl.when(jnp.logical_not(own_place))
            def _():
                copy.start()

            @pl.when(own_place)
            def _():
                pltpu.make_async_copy(made.at[j, rows], held.at[q, j, rows], rs2.at[q, u]).start()

    def handed_out(q, j):
        for u in range(SUB):
            copy, own_place, _ = hand_copy(q, j, u)

            @pl.when(jnp.logical_not(own_place))
            def _():
                copy.wait_send()

    def relay_copy(j, device):
        return pltpu.make_async_remote_copy(
            made.at[j], made.at[j], ss1.at[j, 0], rs1.at[j], device_id=device, device_id_type=MESH
        )

    @pl.when(is_source)
    def _():
        load.wait()
        high, low = wanted(source_q)
        fill_onehot(low)

        def chunk_at(pos):
            return jnp.where(source_q == 2, (pos + 8) % 16, pos)

        def prepare(pos, _):
            j = chunk_at(pos)
            mask = jnp.where(high == j, 1.0, 0.0).astype(jnp.bfloat16)
            block = lax.dot_general(
                onehot[...], own[...] * mask, (((1,), (1,)), ((), ())), preferred_element_type=jnp.float32
            )
            made[j, :BLK, :] = block.astype(jnp.bfloat16)
            made[j, BLK:, :] = pole[...]
            return 0

        def to_holders(pos, _):
            hand_out(source_q, chunk_at(pos))
            return 0

        def to_relay(pos, _):
            relay_copy(pos, relay_of(pos % 8)).start()
            return 0

        lax.fori_loop(0, AHEAD, prepare, 0)
        pl.semaphore_wait(barrier, greeted)

        @pl.when(source_q != 1)
        def _():
            lax.fori_loop(0, 8, to_holders, 0)
            lax.fori_loop(AHEAD, 16, prepare, 0)
            pl.semaphore_wait(ready, answers)
            lax.fori_loop(8, 16, to_holders, 0)

        @pl.when(source_q == 1)
        def _():
            lax.fori_loop(0, AHEAD, to_relay, 0)

            def both(pos, _):
                prepare(pos, 0)
                to_relay(pos, 0)
                return 0

            lax.fori_loop(AHEAD, 16, both, 0)

    @pl.when(jnp.logical_not(is_source))
    def _():
        pl.semaphore_wait(barrier, greeted)

    @pl.when(late)
    def _():
        def answer_holder(i, _):
            device, _, is_late = holder_of_mine(i)

            @pl.when(jnp.logical_not(is_late))
            def _():
                say_ready(device)

            return 0

        lax.fori_loop(0, NQ * SUB, answer_holder, 0)

        @pl.when(is_holder)
        def _():
            say_ready(giver_of_mine())

        for to, back, dz in pairs:
            if dz != 0:

                @pl.when(z == (4 if dz > 0 else 7))
                def _():
                    say_ready(back)

    @pl.when(z == 0)
    def _():
        pl.semaphore_wait(ready, 5)

    for s in range(NQ):
        target_copy(s).start()

    def part_copy(s, u, slot, device):
        n = ROWS + (EXTRA if u == SUB - 1 else 0)
        rows = pl.ds(u * ROWS, n)
        return pltpu.make_async_remote_copy(
            held.at[s, mine, rows], held.at[s, mine, rows], ss2.at[slot], rs2.at[s, u],
            device_id=device, device_id_type=MESH,
        )

    @pl.when(is_relay)
    def _():
        def pass_on(i, _):
            j = 2 * relay_no + i % 2 + 8 * (i // 2)

            @pl.when(i == 2)
            def _():
                pl.semaphore_wait(ready, answers)

            relay_copy(j, sibling).wait_recv()
            hand_out(1, j)
            return 0

        lax.fori_loop(0, 4, pass_on, 0)

    def give(base):
        for u in range(SUB):

            @pl.when(x == u)
            def _():
                def one(i, _):
                    part_copy(held_q, u, 4 * base + i, peer(i, base)).start()
                    return 0

                lax.fori_loop(jnp.where(late == (base == 4), 1, 0), 16, one, 0)

    @pl.when(is_holder)
    def _():
        for u in range(SUB):

            @pl.when(x == u)
            def _():
                part_copy(held_q, u, 0, sibling).wait_recv()

        give(0)

    @pl.when((z == 3) | (is_holder & early & jnp.logical_not(gives)))
    def _():
        pl.semaphore_wait(ready, answers)

    @pl.when(is_holder)
    def _():
        give(4)

    def permute_target(s, _):
        high, low = wanted(s)
        fill_onehot(low)
        pltpu.make_async_remote_copy(
            sent, tgt.at[s], sst.at[s], rst.at[s], device_id=sibling, device_id_type=MESH
        ).wait_recv()
        t = jnp.concatenate([tgt[s, :8, :half], tgt[s, 8:, :half]], axis=1).astype(jnp.float32)
        rows = jnp.concatenate([jnp.where(high == j, t, 0.0).astype(jnp.bfloat16) for j in range(16)], axis=0)
        ordered = lax.dot_general(
            rows, onehot[...], (((1,), (1,)), ((), ())), preferred_element_type=jnp.float32
        )
        for j in range(16):
            moved[s, j] = ordered[8 * j : 8 * j + 8, :]
        return 0

    def prepare_work():
        lax.fori_loop(0, NQ, permute_target, 0)
        total[...] = jnp.zeros_like(total)

    def way_to(s, t):
        if isinstance(s, int) or len(set(WAY[t])) == 1:
            return chip(*WAY[t][s if isinstance(s, int) else 0])
        return chip(*(sum(jnp.where(s == q, WAY[t][q][a], 0) for q in range(NQ)) for a in range(3)))

    def near_copy(s, t):
        return pltpu.make_async_remote_copy(
            held.at[s, mine, pl.ds(0, BLK)], held.at[s, mine, pl.ds(0, BLK)], ss3.at[s, t], rs3.at[s, cls],
            device_id=way_to(s, t), device_id_type=MESH,
        )

    def chunk_in(s, k, sem):
        j = k + 8 * c
        return pltpu.make_async_remote_copy(
            held.at[s, j, pl.ds(0, BLK)], held.at[s, j, pl.ds(0, BLK)], ss3.at[0, 0], sem,
            device_id=sibling, device_id_type=MESH,
        )

    def side_copy(s, k):
        j = k + 8 * c
        return pltpu.make_async_remote_copy(
            held.at[s, j, pl.ds(0, BLK)], held.at[s, j, pl.ds(0, BLK)], ss4.at[s, k], rs4.at[s, k],
            device_id=sibling, device_id_type=MESH,
        )

    def side_in(s, k):
        j = k + 8 * (1 - c)
        return pltpu.make_async_remote_copy(
            held.at[s, j, pl.ds(0, BLK)], held.at[s, j, pl.ds(0, BLK)], ss4.at[s, k], rs4.at[s, k],
            device_id=sibling, device_id_type=MESH,
        )

    def spread(s):
        for u in range(SUB):

            @pl.when(jnp.logical_not(is_holder & (held_q == s) & (x == u)))
            def _():
                part_copy(s, u, 0, sibling).wait_recv()

        for t in range(7):
            near_copy(s, t).start()

    def make_factor(s):
        freq = held[s, mine, BLK : BLK + EXTRA, :].astype(jnp.float32)
        f, w = freq[0:1, :], freq[1:2, :]
        wf, ff = w * f, f * f
        e = tgt[s, :, half:].astype(jnp.float32)
        lvl = level[...]
        for m in range(8):
            gap = e[m : m + 1, :] - lvl
            gap = gap * gap
            gap = jnp.concatenate([gap, gap], axis=1)
            factor[s, m * 128 : m * 128 + 128, :] = wf / (ff + gap)

    def work(s, j):
        w = waves[:, pl.ds(pl.multiple_of(j * BLK, BLK), BLK)].astype(jnp.float32)
        t = moved[s, j]
        pair = jnp.concatenate([(t[m : m + 1, :] * w).astype(jnp.bfloat16) for m in range(8)], axis=0)
        total[s] += jnp.dot(pair, held[s, j, :BLK, :], preferred_element_type=jnp.float32)

    def spread_all():
        def one(i, _):
            spread((i + 2 * c) % 3)
            return 0

        lax.fori_loop(0, NQ, one, 0)

    prepare_work()
    spread_all()
    for s in range(NQ):
        make_factor(s)

    def turn(i, _):
        s = (i + 2 * c) % 3
        other = (i + 2 - 2 * c) % 3

        def arrive(k, _):
            k = (cls + k) % 8

            @pl.when(k != cls)
            def _():
                chunk_in(s, k, rs3.at[s, k]).wait_recv()

            side_copy(s, k).start()
            work(s, k + 8 * c)
            return 0

        def arrive_side(k, _):
            k = (cls + k) % 8
            side_in(other, k).wait_recv()
            work(other, k + 8 * (1 - c))
            return 0

        lax.fori_loop(0, 8, arrive, 0)
        lax.fori_loop(0, 8, arrive_side, 0)
        return 0

    lax.fori_loop(0, NQ, turn, 0)

    def answer_copy(s):
        return pltpu.make_async_remote_copy(
            answer.at[s], part.at[s], ssr.at[s], rsr.at[s], device_id=shifted(QSTEPS[s], 1), device_id_type=MESH
        )

    for s in range(NQ):
        for m in range(8):
            rows = slice(m * 128, m * 128 + 128)
            proj = total[s, rows, :]
            answer[s, m : m + 1, :] = jnp.sum(proj * proj * factor[s, rows, :], axis=0, keepdims=True)
        answer_copy(s).start()

    for s in range(NQ):
        target_copy(s).wait_send()
        for t in range(7):
            near_copy(s, t).wait_send()

    def side_left(k, _):
        for s in range(NQ):
            side_copy(s, k).wait_send()
        return 0

    lax.fori_loop(0, 8, side_left, 0)

    @pl.when(is_holder)
    def _():
        for u in range(SUB):

            @pl.when(x == u)
            def _():
                def left(i, _):
                    @pl.when(i != jnp.where(late, 16, 0))
                    def _():
                        part_copy(held_q, u, i, sibling).wait_send()

                    return 0

                lax.fori_loop(0, 32, left, 0)

    @pl.when(is_source & (source_q != 1))
    def _():
        def left(j, _):
            handed_out(source_q, j)
            return 0

        lax.fori_loop(0, 16, left, 0)

    @pl.when(is_source & (source_q == 1))
    def _():
        def left(j, _):
            relay_copy(j, sibling).wait_send()
            return 0

        lax.fori_loop(0, 16, left, 0)

    @pl.when(is_relay)
    def _():
        def left(i, _):
            handed_out(1, 2 * relay_no + i % 2 + 8 * (i // 2))
            return 0

        lax.fori_loop(0, 4, left, 0)

    for s in range(NQ):
        answer_copy(s).wait()
    out[...] = (part[0] + part[1] + part[2]) * (1.0 / 128.0)


def local(target, target_energy, waves, band_energy, occupation, gmap, pole_vectors, pole_freq, pole_weight):
    tgt = target[0, 0, 0]
    vmem = pl.BlockSpec(memory_space=pltpu.VMEM)
    dma = pltpu.SemaphoreType.DMA
    out = pl.pallas_call(
        kernel,
        out_shape=jax.ShapeDtypeStruct((8, 256), jnp.float32),
        in_specs=[vmem, pl.BlockSpec(memory_space=pl.ANY)] + [vmem] * 7,
        out_specs=vmem,
        scratch_shapes=[
            pltpu.VMEM((NQ, 16, BLK + EXTRA, 256), jnp.bfloat16),
            pltpu.VMEM((16, BLK + EXTRA, 256), jnp.bfloat16),
            pltpu.VMEM((BLK, 4096), jnp.bfloat16),
            pltpu.VMEM((256, 4096), jnp.bfloat16),
            pltpu.VMEM((16, 2048 + 128), jnp.bfloat16),
            pltpu.VMEM((NQ, 16, 2048 + 128), jnp.bfloat16),
            pltpu.VMEM((NQ, 16, 8, BLK), jnp.float32),
            pltpu.VMEM((NQ, 1024, 256), jnp.float32),
            pltpu.VMEM((NQ, 1024, 256), jnp.float32),
            pltpu.VMEM((NQ, 8, 256), jnp.float32),
            pltpu.VMEM((NQ, 8, 256), jnp.float32),
            pltpu.VMEM((128, 128), jnp.float32),
            pltpu.VMEM((EXTRA, 256), jnp.bfloat16),
            dma,
            dma((16, SUB)),
            dma((32,)),
            dma((NQ, 7)),
            dma((NQ, 8)),
            dma((NQ,)),
            dma((NQ,)),
            dma((16,)),
            dma((NQ, SUB)),
            dma((NQ, 8)),
            dma((NQ, 8)),
            dma((NQ,)),
            dma((NQ,)),
            pltpu.SemaphoreType.REGULAR,
        ],
        compiler_params=pltpu.CompilerParams(
            collective_id=0, has_side_effects=True, vmem_limit_bytes=56 << 20
        ),
    )(
        gmap, pole_vectors[0, 0, 0], waves[0, 0, 0], tgt, target_energy[0, 0], band_energy[0, 0],
        occupation[0, 0], pole_freq[0, 0], pole_weight[0, 0],
    )
    return out[None, None, None]


def solution(mesh):
    cut = P("kx", "ky", "kz", None, None)
    row = P("kx", "ky", "kz", None)
    return jax.shard_map(
        local,
        mesh=mesh,
        in_specs=(cut, row, cut, row, row, P(), cut, row, row),
        out_specs=cut,
        check_vma=False,
    )
```

time: 97.9 us -> 87.9 us (0.90)
  the two profiles are of different devices: /device:TPU:1 before, /device:TPU:9 now
where the time goes in v2:
time: 87.9 us; the launch traced here: 87.7 us
  Pallas kernels  86.4 us (98%)
  local copies, waits for them, and re-layouts  1.3 us (1%)
    pallas_call x1, Pallas kernels, local(): pl.pallas_call(kernel, out_shape=jax.ShapeDtypeStruct((8, 256), jnp.float...  86.4 us

profile of v2, /device:TPU:9, one launch (start us, length us, event | category | flops | bytes accessed | tf_op | source)
XLA Modules:
  0.0 87.7 jit_solution(4780294760375776438)
XLA Ops:
  0.0 86.4 %shard_map.91 = f32[8,256]{1,0:T(8,128)} custom-call(s32[3,4096]{1,0:T(4,128)} %gmap.1, bf16[256,4096]{1,0:T(8,128)(2,1)} %bitcast.9, bf16[128,4096]{1,0:T(8,128)(2,1)} %bitcast.10, bf16[8,4096]{1,0:T(8,128)(2,1)} %bitcast.11, bf16[1,8]{1,0:T(2,128)(2,1)} %bitcast.15, f32[1,128]{1,0:T(1,128)} %bitcast.16, s32[1,128]{1,0:T(1,128)} %bitcast.17, ...), custom_call_target="tpu_custom_call" | custom-call | tf_op jit(solution)/shard_map/pallas_call | solution.py:583
  86.4 1.3 %copy.11 = f32[1,1,1,8,256]{4,3,2,1,0:T(8,128)} copy(f32[1,1,1,8,256]{4,3,2,1,0:T(8,128)} %bitcast.12) | data formatting | bytes 16384

commit v3 on v2

--- a/solution.py
+++ b/solution.py
@@ -11,12 +11,13 @@
 QSTEPS = ((1, 0, 0), (1, 1, 0), (1, 1, 1))
 NQ = 3
 BLK = 256
-SUB = 4
+SUB = 2
 ROWS = BLK // SUB
-AHEAD = 8
+AHEAD = 12
 EXTRA = 16
 NEAR = {1: (0, 1, 0), 2: (1, 0, 0), 3: (0, 0, 1), 5: (0, 0, -1), 6: (-1, 0, 0), 7: (0, -1, 0)}
 FAR = ((2, 0, 0), (0, 1, 1), (0, -1, -1))
+ACROSS = ((1, 1, -1), (0, 1, -3), (0, -1, 3), (-1, -1, 1))
 WAY = [[FAR[s] if t == 4 else NEAR[t] for s in range(NQ)] for t in range(1, 8)]
 
 
@@ -32,7 +33,7 @@
 def kernel(
     gmap, vecs, waves, target, energy_row, band_energy, occupation, freq_row, weight_row, out,
     held, made, onehot, own, sent, tgt, moved, total, factor, answer, part, level, pole,
-    own_sem, ss1, ss2, ss3, ss4, sst, ssr, rs1, rs2, rs3, rs4, rst, rsr, ready,
+    own_sem, ss1, ss2, ss5, rs5, ss3, ss4, sst, ssr, rs1, rs2, rs3, rs4, rst, rsr, ready,
 ):
     me = tuple(lax.axis_index(a) for a in ("kx", "ky", "kz"))
     x, y, z, c = chip_of(me)
@@ -50,15 +51,11 @@
     source_q = jnp.where(x == 0, c, 2)
     late = z >= 4
     early = jnp.logical_not(late)
-    held_at = (z + 7 - 4 * c) % 8
-    held_q = jnp.minimum(held_at // 2, 2)
-    is_holder = (held_at == 0) | (held_at == 2) | (held_at == 5)
+    held_q = jnp.clip(z - 1, 0, 2)
+    held_u = x % 2
+    is_holder = (z >= 1) & (z <= 3) & (x // 2 == c)
     relay_no = jnp.where(z == 2, 3 - c, jnp.where(x == 3, 0, 1))
     is_relay = (y == 0) & (((x == 0) & (z == 2)) | ((z == 1) & (((x == 3) & (c == 1)) | ((x == 1) & (c == 0)))))
-    gives = (is_source & (source_q != 1)) | is_relay
-
-    def first_z(s, core):
-        return (1 + 2 * s + s // 2 + 4 * core) % 8
 
     def relay_of(k):
         r = k // 2
@@ -73,12 +70,14 @@
         return device_of(jnp.where(s == 2, 1, 0), 0, 1, jnp.where(s == 0, 0, 1))
 
     def holder_of(s, u, k, core):
-        hz = first_z(s, core)
-        return u, (k + 48 - 2 * u - 3 * hz) % 8, hz
-
-    def giver_of_mine():
-        to_relay = held_q == 1
-        return tuple(jnp.where(to_relay, a, b) for a, b in zip(relay_of(cls), source_of(held_q)))
+        hx, hz = 2 * core + u, 1 + s
+        return hx, (k + 48 - 2 * hx - 3 * hz) % 8, hz
+
+    giver = tuple(jnp.where(held_q == 1, a, b) for a, b in zip(relay_of(cls), source_of(held_q)))
+    from_other = is_holder & ((giver[0] != me[0]) | (giver[1] != me[1]) | (giver[2] != me[2]))
+    by_z = [(z == i) | (z == j) for i, j in enumerate((7, 6, 5, 4))]
+    side = jnp.where(late, -1, 1)
+    partner = chip(*(side * sum(jnp.where(b, way[a], 0) for b, way in zip(by_z, ACROSS)) for a in range(3)))
 
     barrier = pltpu.get_barrier_semaphore()
 
@@ -109,56 +108,34 @@
                 hello(to)
 
     def holder_of_mine(i):
-        u, hy, hz = holder_of(i // 4, i % 4, cls, c)
-        return device_of(u, hy, hz, c), (u == x) & (hz == z), hz >= 4
+        hx, hy, hz = holder_of(i // 2, i % 2, cls, c)
+        return device_of(hx, hy, hz, c), (hx == x) & (hz == z)
 
     def greet(i, _):
-        device, own_place, is_late = holder_of_mine(i)
-
-        @pl.when(jnp.logical_not(own_place) & (early | is_late))
+        device, own_place = holder_of_mine(i)
+
+        @pl.when(jnp.logical_not(own_place))
         def _():
             hello(device)
 
         return 0
 
-    def peer(i, base):
-        px, pz = (x + i) % 4, base + (z + i // 4) % 4
+    def peer(i):
+        px, pz = (x + i) % 4, (z + i // 4) % 4
         return device_of(px, (cls + 48 - 2 * px - 3 * pz) % 8, pz, c)
 
-    lax.fori_loop(0, NQ * SUB, greet, 0)
-
-    @pl.when(is_holder & early)
-    def _():
-        @pl.when(jnp.logical_not(is_source & (source_q == 0)))
-        def _():
-            hello(giver_of_mine())
-
-        def greet_late(i, _):
-            hello(peer(i, 4))
-            return 0
-
-        lax.fori_loop(0, 16, greet_late, 0)
+    @pl.when(early)
+    def _():
+        lax.fori_loop(0, NQ * SUB, greet, 0)
+        hello(partner)
+
+    @pl.when(from_other)
+    def _():
+        hello(giver)
 
     @pl.when(is_relay)
     def _():
         hello(source_of(1))
-
-    def given_to(i):
-        q = jnp.where(is_relay, 1, source_q)
-        core = jnp.where(q == 2, 0, 1)
-        k = jnp.where(is_relay, 2 * relay_no, 0) + i // 4
-        u, hy, hz = holder_of(q, i % 4, k, core)
-        return device_of(u, hy, hz, core)
-
-    many = jnp.where(is_relay, 8, 32)
-
-    @pl.when(gives)
-    def _():
-        def greet_given(i, _):
-            hello(given_to(i))
-            return 0
-
-        lax.fori_loop(0, many, greet_given, 0)
 
     load = pltpu.make_async_copy(vecs, own, own_sem)
 
@@ -194,22 +171,16 @@
 
     edge = (z == 0) | (z == 3)
     peers = 2 * NQ + 1 + 9
-    first_held = jnp.where(c == 0, 8, 4)
     greeted_early = (
         peers
         - jnp.where(edge, 5, 0)
         + jnp.where(is_holder, 15, 0)
-        + jnp.where(is_relay, 8, 0)
+        + jnp.where(is_relay, 8 - jnp.where(relay_no == 3, 1, 0), 0)
         + jnp.where(is_source, jnp.where(source_q == 0, 31, jnp.where(source_q == 1, 4, 32)), 0)
     )
-    greeted_late = (
-        peers
-        + jnp.where((z == 4) | (z == 7), 5, 0)
-        + first_held
-        + jnp.where(is_holder, 32, 0)
-    )
+    greeted_late = peers + jnp.where((z == 4) | (z == 7), 5, 0) + 1
     greeted = jnp.where(late, greeted_late, greeted_early)
-    answers = jnp.where(edge, 5, 0) + jnp.where(is_holder, 16, 0) + jnp.where(gives, many, 0)
+    answers = jnp.where(edge, 5, 0) + 1
 
     def target_copy(s):
         return pltpu.make_async_remote_copy(
@@ -262,7 +233,7 @@
         fill_onehot(low)
 
         def chunk_at(pos):
-            return jnp.where(source_q == 2, (pos + 8) % 16, pos)
+            return pos // 2 + 8 * (pos % 2)
 
         def prepare(pos, _):
             j = chunk_at(pos)
@@ -274,34 +245,28 @@
             made[j, BLK:, :] = pole[...]
             return 0
 
-        def to_holders(pos, _):
-            hand_out(source_q, chunk_at(pos))
-            return 0
-
-        def to_relay(pos, _):
-            relay_copy(pos, relay_of(pos % 8)).start()
+        def send(pos, _):
+            j = chunk_at(pos)
+
+            @pl.when(source_q == 1)
+            def _():
+                relay_copy(j, relay_of(j % 8)).start()
+
+            @pl.when(source_q != 1)
+            def _():
+                hand_out(source_q, j)
+
+            return 0
+
+        def both(pos, _):
+            prepare(pos, 0)
+            send(pos, 0)
             return 0
 
         lax.fori_loop(0, AHEAD, prepare, 0)
         pl.semaphore_wait(barrier, greeted)
-
-        @pl.when(source_q != 1)
-        def _():
-            lax.fori_loop(0, 8, to_holders, 0)
-            lax.fori_loop(AHEAD, 16, prepare, 0)
-            pl.semaphore_wait(ready, answers)
-            lax.fori_loop(8, 16, to_holders, 0)
-
-        @pl.when(source_q == 1)
-        def _():
-            lax.fori_loop(0, AHEAD, to_relay, 0)
-
-            def both(pos, _):
-                prepare(pos, 0)
-                to_relay(pos, 0)
-                return 0
-
-            lax.fori_loop(AHEAD, 16, both, 0)
+        lax.fori_loop(0, AHEAD, send, 0)
+        lax.fori_loop(AHEAD, 16, both, 0)
 
     @pl.when(jnp.logical_not(is_source))
     def _():
@@ -309,21 +274,7 @@
 
     @pl.when(late)
     def _():
-        def answer_holder(i, _):
-            device, _, is_late = holder_of_mine(i)
-
-            @pl.when(jnp.logical_not(is_late))
-            def _():
-                say_ready(device)
-
-            return 0
-
-        lax.fori_loop(0, NQ * SUB, answer_holder, 0)
-
-        @pl.when(is_holder)
-        def _():
-            say_ready(giver_of_mine())
-
+        say_ready(partner)
         for to, back, dz in pairs:
             if dz != 0:
 
@@ -333,7 +284,7 @@
 
     @pl.when(z == 0)
     def _():
-        pl.semaphore_wait(ready, 5)
+        pl.semaphore_wait(ready, answers)
 
     for s in range(NQ):
         target_copy(s).start()
@@ -349,46 +300,26 @@
     @pl.when(is_relay)
     def _():
         def pass_on(i, _):
-            j = 2 * relay_no + i % 2 + 8 * (i // 2)
-
-            @pl.when(i == 2)
-            def _():
-                pl.semaphore_wait(ready, answers)
-
+            j = 2 * relay_no + i // 2 + 8 * (i % 2)
             relay_copy(j, sibling).wait_recv()
             hand_out(1, j)
             return 0
 
         lax.fori_loop(0, 4, pass_on, 0)
 
-    def give(base):
+    @pl.when(is_holder)
+    def _():
         for u in range(SUB):
 
-            @pl.when(x == u)
-            def _():
-                def one(i, _):
-                    part_copy(held_q, u, 4 * base + i, peer(i, base)).start()
+            @pl.when(held_u == u)
+            def _():
+                part_copy(held_q, u, 0, sibling).wait_recv()
+
+                def give(i, _):
+                    part_copy(held_q, u, i, peer(i)).start()
                     return 0
 
-                lax.fori_loop(jnp.where(late == (base == 4), 1, 0), 16, one, 0)
-
-    @pl.when(is_holder)
-    def _():
-        for u in range(SUB):
-
-            @pl.when(x == u)
-            def _():
-                part_copy(held_q, u, 0, sibling).wait_recv()
-
-        give(0)
-
-    @pl.when((z == 3) | (is_holder & early & jnp.logical_not(gives)))
-    def _():
-        pl.semaphore_wait(ready, answers)
-
-    @pl.when(is_holder)
-    def _():
-        give(4)
+                lax.fori_loop(1, 16, give, 0)
 
     def permute_target(s, _):
         high, low = wanted(s)
@@ -441,12 +372,25 @@
             device_id=sibling, device_id_type=MESH,
         )
 
+    def across_copy(s):
+        return pltpu.make_async_remote_copy(
+            held.at[s, mine], held.at[s, mine], ss5.at[s], rs5.at[s], device_id=partner, device_id_type=MESH
+        )
+
     def spread(s):
-        for u in range(SUB):
-
-            @pl.when(jnp.logical_not(is_holder & (held_q == s) & (x == u)))
-            def _():
-                part_copy(s, u, 0, sibling).wait_recv()
+        @pl.when(late)
+        def _():
+            across_copy(s).wait_recv()
+
+        @pl.when(early)
+        def _():
+            for u in range(SUB):
+
+                @pl.when(jnp.logical_not(is_holder & (held_q == s) & (held_u == u)))
+                def _():
+                    part_copy(s, u, 0, sibling).wait_recv()
+
+            across_copy(s).start()
 
         for t in range(7):
             near_copy(s, t).start()
@@ -471,19 +415,23 @@
 
     def spread_all():
         def one(i, _):
-            spread((i + 2 * c) % 3)
+            spread((2 * i) % 3)
             return 0
 
         lax.fori_loop(0, NQ, one, 0)
 
     prepare_work()
+
+    @pl.when(early & (z != 0))
+    def _():
+        pl.semaphore_wait(ready, answers)
+
     spread_all()
     for s in range(NQ):
         make_factor(s)
 
     def turn(i, _):
-        s = (i + 2 * c) % 3
-        other = (i + 2 - 2 * c) % 3
+        s = (2 * i) % 3
 
         def arrive(k, _):
             k = (cls + k) % 8
@@ -498,8 +446,8 @@
 
         def arrive_side(k, _):
             k = (cls + k) % 8
-            side_in(other, k).wait_recv()
-            work(other, k + 8 * (1 - c))
+            side_in(s, k).wait_recv()
+            work(s, k + 8 * (1 - c))
             return 0
 
         lax.fori_loop(0, 8, arrive, 0)
@@ -532,20 +480,22 @@
 
     lax.fori_loop(0, 8, side_left, 0)
 
+    @pl.when(early)
+    def _():
+        for s in range(NQ):
+            across_copy(s).wait_send()
+
     @pl.when(is_holder)
     def _():
         for u in range(SUB):
 
-            @pl.when(x == u)
+            @pl.when(held_u == u)
             def _():
                 def left(i, _):
-                    @pl.when(i != jnp.where(late, 16, 0))
-                    def _():
-                        part_copy(held_q, u, i, sibling).wait_send()
-
+                    part_copy(held_q, u, i, sibling).wait_send()
                     return 0
 
-                lax.fori_loop(0, 32, left, 0)
+                lax.fori_loop(1, 16, left, 0)
 
     @pl.when(is_source & (source_q != 1))
     def _():
@@ -566,7 +516,7 @@
     @pl.when(is_relay)
     def _():
         def left(i, _):
-            handed_out(1, 2 * relay_no + i % 2 + 8 * (i // 2))
+            handed_out(1, 2 * relay_no + i // 2 + 8 * (i % 2))
             return 0
 
         lax.fori_loop(0, 4, left, 0)
@@ -601,7 +551,9 @@
             pltpu.VMEM((EXTRA, 256), jnp.bfloat16),
             dma,
             dma((16, SUB)),
-            dma((32,)),
+            dma((16,)),
+            dma((NQ,)),
+            dma((NQ,)),
             dma((NQ, 7)),
             dma((NQ, 8)),
             dma((NQ,)),

time: 87.9 us -> 92.7 us (1.055)
  the two profiles are of different devices: /device:TPU:9 before, /device:TPU:6 now
where the time goes in v3:
time: 92.7 us; the launch traced here: 92.5 us
  Pallas kernels  91.2 us (98%)
  local copies, waits for them, and re-layouts  1.3 us (1%)
    pallas_call x1, Pallas kernels, local(): pl.pallas_call(kernel, out_shape=jax.ShapeDtypeStruct((8, 256), jnp.float...  91.2 us

profile of v3, /device:TPU:6, one launch (start us, length us, event | category | flops | bytes accessed | tf_op | source)
XLA Modules:
  0.0 92.5 jit_solution(8027574818177391900)
XLA Ops:
  0.0 91.2 %shard_map.91 = f32[8,256]{1,0:T(8,128)} custom-call(s32[3,4096]{1,0:T(4,128)} %gmap.1, bf16[256,4096]{1,0:T(8,128)(2,1)} %bitcast.9, bf16[128,4096]{1,0:T(8,128)(2,1)} %bitcast.10, bf16[8,4096]{1,0:T(8,128)(2,1)} %bitcast.11, bf16[1,8]{1,0:T(2,128)(2,1)} %bitcast.15, f32[1,128]{1,0:T(1,128)} %bitcast.16, s32[1,128]{1,0:T(1,128)} %bitcast.17, ...), custom_call_target="tpu_custom_call" | custom-call | tf_op jit(solution)/shard_map/pallas_call | solution.py:533
  91.2 1.3 %copy.11 = f32[1,1,1,8,256]{4,3,2,1,0:T(8,128)} copy(f32[1,1,1,8,256]{4,3,2,1,0:T(8,128)} %bitcast.12) | data formatting | bytes 16384

commit v4 on v2

--- a/solution.py
+++ b/solution.py
@@ -159,38 +159,6 @@
             return 0
 
         lax.fori_loop(0, many, greet_given, 0)
-
-    load = pltpu.make_async_copy(vecs, own, own_sem)
-
-    @pl.when(is_source)
-    def _():
-        load.start()
-
-    def wanted(q):
-        row = gmap[pl.ds(q, 1), :]
-        return row // BLK, row % BLK
-
-    def fill_onehot(low):
-        for r in range(0, BLK, 32):
-            rows = lax.broadcasted_iota(jnp.int32, (32, low.shape[1]), 0) + r
-            onehot[r : r + 32, :] = jnp.where(rows == low, 1.0, 0.0).astype(jnp.bfloat16)
-
-    half = target.shape[1] // 2
-    for h in range(2):
-        sent[8 * h : 8 * h + 8, :half] = target[:, h * half : h * half + half].astype(jnp.float32).astype(jnp.bfloat16)
-    spot = lax.broadcasted_iota(jnp.int32, (8, 8), 0) == lax.broadcasted_iota(jnp.int32, (8, 8), 1)
-    spot = jnp.where(spot, jnp.broadcast_to(energy_row[...].astype(jnp.float32), (8, 8)), 0.0)
-    spot = jnp.broadcast_to(jnp.sum(spot, axis=1, keepdims=True), (8, 128))
-    sent[:, half:] = jnp.concatenate([spot, spot], axis=0).astype(jnp.bfloat16)
-    lvl_row = band_energy[...] - (2 * occupation[...] - 1).astype(jnp.float32)
-    lvl_row = lvl_row.astype(jnp.bfloat16).astype(jnp.float32)
-    level[...] = jnp.broadcast_to(lvl_row, (128, 128)).T
-    row_at = lax.broadcasted_iota(jnp.int32, (EXTRA, 256), 0)
-    pole[...] = jnp.where(
-        row_at == 0,
-        freq_row[...].astype(jnp.float32),
-        jnp.where(row_at == 1, weight_row[...].astype(jnp.float32), 0.0),
-    ).astype(jnp.bfloat16)
 
     edge = (z == 0) | (z == 3)
     peers = 2 * NQ + 1 + 9
@@ -211,6 +179,64 @@
     greeted = jnp.where(late, greeted_late, greeted_early)
     answers = jnp.where(edge, 5, 0) + jnp.where(is_holder, 16, 0) + jnp.where(gives, many, 0)
 
+    @pl.when(late)
+    def _():
+        pl.semaphore_wait(barrier, greeted)
+
+        @pl.when(is_holder)
+        def _():
+            say_ready(giver_of_mine())
+
+        def answer_holder(i, _):
+            device, _, is_late = holder_of_mine(i)
+
+            @pl.when(jnp.logical_not(is_late))
+            def _():
+                say_ready(device)
+
+            return 0
+
+        lax.fori_loop(0, NQ * SUB, answer_holder, 0)
+
+        for to, back, dz in pairs:
+            if dz != 0:
+
+                @pl.when(z == (4 if dz > 0 else 7))
+                def _():
+                    say_ready(back)
+
+    load = pltpu.make_async_copy(vecs, own, own_sem)
+
+    @pl.when(is_source)
+    def _():
+        load.start()
+
+    def wanted(q):
+        row = gmap[pl.ds(q, 1), :]
+        return row // BLK, row % BLK
+
+    def fill_onehot(low):
+        for r in range(0, BLK, 32):
+            rows = lax.broadcasted_iota(jnp.int32, (32, low.shape[1]), 0) + r
+            onehot[r : r + 32, :] = jnp.where(rows == low, 1.0, 0.0).astype(jnp.bfloat16)
+
+    half = target.shape[1] // 2
+    for h in range(2):
+        sent[8 * h : 8 * h + 8, :half] = target[:, h * half : h * half + half].astype(jnp.float32).astype(jnp.bfloat16)
+    spot = lax.broadcasted_iota(jnp.int32, (8, 8), 0) == lax.broadcasted_iota(jnp.int32, (8, 8), 1)
+    spot = jnp.where(spot, jnp.broadcast_to(energy_row[...].astype(jnp.float32), (8, 8)), 0.0)
+    spot = jnp.broadcast_to(jnp.sum(spot, axis=1, keepdims=True), (8, 128))
+    sent[:, half:] = jnp.concatenate([spot, spot], axis=0).astype(jnp.bfloat16)
+    lvl_row = band_energy[...] - (2 * occupation[...] - 1).astype(jnp.float32)
+    lvl_row = lvl_row.astype(jnp.bfloat16).astype(jnp.float32)
+    level[...] = jnp.broadcast_to(lvl_row, (128, 128)).T
+    row_at = lax.broadcasted_iota(jnp.int32, (EXTRA, 256), 0)
+    pole[...] = jnp.where(
+        row_at == 0,
+        freq_row[...].astype(jnp.float32),
+        jnp.where(row_at == 1, weight_row[...].astype(jnp.float32), 0.0),
+    ).astype(jnp.bfloat16)
+
     def target_copy(s):
         return pltpu.make_async_remote_copy(
             sent, tgt.at[s], sst.at[s], rst.at[s], device_id=shifted(QSTEPS[s], -1), device_id_type=MESH
@@ -303,33 +329,9 @@
 
             lax.fori_loop(AHEAD, 16, both, 0)
 
-    @pl.when(jnp.logical_not(is_source))
+    @pl.when(early & jnp.logical_not(is_source))
     def _():
         pl.semaphore_wait(barrier, greeted)
-
-    @pl.when(late)
-    def _():
-        def answer_holder(i, _):
-            device, _, is_late = holder_of_mine(i)
-
-            @pl.when(jnp.logical_not(is_late))
-            def _():
-                say_ready(device)
-
-            return 0
-
-        lax.fori_loop(0, NQ * SUB, answer_holder, 0)
-
-        @pl.when(is_holder)
-        def _():
-            say_ready(giver_of_mine())
-
-        for to, back, dz in pairs:
-            if dz != 0:
-
-                @pl.when(z == (4 if dz > 0 else 7))
-                def _():
-                    say_ready(back)
 
     @pl.when(z == 0)
     def _():
@@ -464,14 +466,14 @@
             factor[s, m * 128 : m * 128 + 128, :] = wf / (ff + gap)
 
     def work(s, j):
-        w = waves[:, pl.ds(pl.multiple_of(j * BLK, BLK), BLK)].astype(jnp.float32)
-        t = moved[s, j]
-        pair = jnp.concatenate([(t[m : m + 1, :] * w).astype(jnp.bfloat16) for m in range(8)], axis=0)
+        w = waves[:, pl.ds(pl.multiple_of(j * BLK, BLK), BLK)]
+        t = moved[s, j].astype(jnp.bfloat16)
+        pair = jnp.concatenate([t[m : m + 1, :] * w for m in range(8)], axis=0)
         total[s] += jnp.dot(pair, held[s, j, :BLK, :], preferred_element_type=jnp.float32)
 
     def spread_all():
         def one(i, _):
-            spread((i + 2 * c) % 3)
+            spread((2 * i) % 3)
             return 0
 
         lax.fori_loop(0, NQ, one, 0)
@@ -481,9 +483,13 @@
     for s in range(NQ):
         make_factor(s)
 
+    def answer_copy(s):
+        return pltpu.make_async_remote_copy(
+            answer.at[s], part.at[s], ssr.at[s], rsr.at[s], device_id=shifted(QSTEPS[s], 1), device_id_type=MESH
+        )
+
     def turn(i, _):
-        s = (i + 2 * c) % 3
-        other = (i + 2 - 2 * c) % 3
+        s = (2 * i) % 3
 
         def arrive(k, _):
             k = (cls + k) % 8
@@ -498,27 +504,25 @@
 
         def arrive_side(k, _):
             k = (cls + k) % 8
-            side_in(other, k).wait_recv()
-            work(other, k + 8 * (1 - c))
+            side_in(s, k).wait_recv()
+            work(s, k + 8 * (1 - c))
             return 0
 
         lax.fori_loop(0, 8, arrive, 0)
         lax.fori_loop(0, 8, arrive_side, 0)
+        for q in range(NQ):
+
+            @pl.when(s == q)
+            def _():
+                for m in range(8):
+                    rows = slice(m * 128, m * 128 + 128)
+                    proj = total[q, rows, :]
+                    answer[q, m : m + 1, :] = jnp.sum(proj * proj * factor[q, rows, :], axis=0, keepdims=True)
+                answer_copy(q).start()
+
         return 0
 
     lax.fori_loop(0, NQ, turn, 0)
-
-    def answer_copy(s):
-        return pltpu.make_async_remote_copy(
-            answer.at[s], part.at[s], ssr.at[s], rsr.at[s], device_id=shifted(QSTEPS[s], 1), device_id_type=MESH
-        )
-
-    for s in range(NQ):
-        for m in range(8):
-            rows = slice(m * 128, m * 128 + 128)
-            proj = total[s, rows, :]
-            answer[s, m : m + 1, :] = jnp.sum(proj * proj * factor[s, rows, :], axis=0, keepdims=True)
-        answer_copy(s).start()
 
     for s in range(NQ):
         target_copy(s).wait_send()

time: 87.9 us -> 85.1 us (0.968)
  the two profiles are of different devices: /device:TPU:9 before, /device:TPU:1 now
where the time goes in v4:
time: 85.1 us; the launch traced here: 84.9 us
  Pallas kernels  83.6 us (98%)
  local copies, waits for them, and re-layouts  1.3 us (2%)
    pallas_call x1, Pallas kernels, local(): pl.pallas_call(kernel, out_shape=jax.ShapeDtypeStruct((8, 256), jnp.float...  83.6 us

profile of v4, /device:TPU:1, one launch (start us, length us, event | category | flops | bytes accessed | tf_op | source)
XLA Modules:
  0.0 84.9 jit_solution(15651651590570185612)
XLA Ops:
  0.0 83.6 %shard_map.91 = f32[8,256]{1,0:T(8,128)} custom-call(s32[3,4096]{1,0:T(4,128)} %gmap.1, bf16[256,4096]{1,0:T(8,128)(2,1)} %bitcast.9, bf16[128,4096]{1,0:T(8,128)(2,1)} %bitcast.10, bf16[8,4096]{1,0:T(8,128)(2,1)} %bitcast.11, bf16[1,8]{1,0:T(2,128)(2,1)} %bitcast.15, f32[1,128]{1,0:T(1,128)} %bitcast.16, s32[1,128]{1,0:T(1,128)} %bitcast.17, ...), custom_call_target="tpu_custom_call" | custom-call | tf_op jit(solution)/shard_map/pallas_call | solution.py:587
  83.6 1.3 %copy.11 = f32[1,1,1,8,256]{4,3,2,1,0:T(8,128)} copy(f32[1,1,1,8,256]{4,3,2,1,0:T(8,128)} %bitcast.12) | data formatting | bytes 16384
